TPU v7x, 32 devices: a whole 2x2x4 slice. The times are simulated.
32 devices in a mesh: gx: 8 (over z, y), gz: 4 (over x, core).
Axes of the slice: x: 2, y: 2, z: 4, core: 2. Of those that a mesh axis runs over, the one named last changes fastest.
Arguments:
- charge: float32 [32, 1024, 1024], P('gz', 'gx'), may hold values from -24 to 24
- cell_permittivity: float32 [32], replicated, may hold values from 1 to 4
- face_permittivity: float32 [32], replicated, may hold values from 1 to 4
- screening: float32 [32], replicated, may hold values from 0.001 to 0.01
Outputs:
- potential: float32 [32, 1024, 1024], P('gz', 'gx')
All inputs are finite; a program needn't handle non-finite values.
Results may differ from a plain program's by a relative error of at most 0.0003.
Values sent between devices are 32-bit elements; how exact they have to be, the bound alone decides.
A program may use at most 128 MiB of HBM per device.

v0:
```python
import functools

import jax
import jax.numpy as jnp
import ml_dtypes
import numpy as np
from jax import lax
from jax.experimental import pallas as pl
from jax.experimental.pallas import tpu as pltpu
from jax.sharding import PartitionSpec as P

f32 = jnp.float32
bf16 = jnp.bfloat16
LANES = 128
ROWS = 8
STEP = 16
CHUNKS = 2


def params():
    return pltpu.CompilerParams(
        vmem_limit_bytes=48 * 1024 * 1024, dimension_semantics=("arbitrary",)
    )


def cost(flops, moved):
    return pl.CostEstimate(flops=flops, bytes_accessed=moved, transcendentals=0)


def frequencies(length):
    col = np.arange(length)
    middle = length // 2
    return np.where(col <= middle, col, col - middle)


def basis_table(length):
    freq = frequencies(length)
    phase = (np.arange(length)[:, None] * freq[None, :]) % length
    angles = phase * (2.0 * np.pi / length)
    cos_part = np.arange(length)[None, :] <= length // 2
    return np.where(cos_part, np.cos(angles), np.sin(angles))


def halves(table):
    high = table.astype(ml_dtypes.bfloat16)
    low = (table - high.astype(np.float64)).astype(ml_dtypes.bfloat16)
    return jnp.asarray(high), jnp.asarray(low)


def mode_weights(length):
    col = np.arange(length)
    edge = (col == 0) | (col == length // 2)
    return np.where(edge, 1.0 / length, 2.0 / length)


def mode_shift(length):
    return (2.0 - 2.0 * np.cos(frequencies(length) * (2.0 * np.pi / length))).astype(np.float32)


def split(value):
    high = value.astype(bf16)
    low = (value - high.astype(f32)).astype(bf16)
    return high, low


def product(left, right):
    dot = functools.partial(jnp.dot, preferred_element_type=f32)
    return dot(left[0], right[0]) + (dot(left[0], right[1]) + dot(left[1], right[0]))


def eigen_kernel(
    cell_col, cell_row, face_col, face_row, low_row, screen_col, screen_row, shift_row,
    ratio_ref, fore_high, fore_low, back_high, back_low,
):
    n = cell_col.shape[0]
    shape = (n, LANES)
    row = lax.broadcasted_iota(jnp.int32, shape, 0)
    col = lax.broadcasted_iota(jnp.int32, shape, 1)
    lane = lax.broadcasted_iota(jnp.int32, (1, LANES), 1)
    unit = (row == col).astype(f32)

    def pairing(parity):
        def lower(index):
            return ((index + parity) % 2 == 0) & (index < n - 1)

        def upper(index):
            return ((index + parity) % 2 == 1) & (index > 0) & (index < n)

        mate = jnp.where(lower(col), col + 1, jnp.where(upper(col), col - 1, -1))
        return (
            (row == mate).astype(f32),
            lower(col),
            lower(row),
            lower(lane),
            lower(lane) | upper(lane),
        )

    pairings = (pairing(0), pairing(1))

    def lane_mates(value, low):
        return jnp.where(low, pltpu.roll(value, LANES - 1, 1), pltpu.roll(value, 1, 1))

    def stage(matrix, vectors, pair):
        mate, low_cols, low_rows, low_lane, paired = pair
        other = lane_mates(matrix, low_cols)
        gap = jnp.sum(mate * other - unit * matrix, axis=0, keepdims=True)
        twice = jnp.sum(mate * matrix + unit * other, axis=0, keepdims=True)
        positive = (gap > 0.0) | ((gap == 0.0) & low_lane)
        size = jnp.abs(gap) + jnp.sqrt(gap * gap + twice * twice) + 1e-30
        tangent = jnp.where(positive, twice, -twice) / size
        square = 1.0 + tangent * tangent
        cosine = lax.rsqrt(square)
        cosine = cosine * (1.5 - 0.5 * square * cosine * cosine)
        own = jnp.where(paired, cosine * tangent, 1.0)
        cross = jnp.where(paired, cosine, 0.0)
        own_col = jnp.sum(unit * own, axis=1, keepdims=True)
        cross_col = jnp.sum(unit * cross, axis=1, keepdims=True)
        vectors = vectors * own + lane_mates(vectors, low_cols) * cross
        matrix = matrix * own + other * cross
        other = jnp.where(low_rows, pltpu.roll(matrix, n - 1, 0), pltpu.roll(matrix, 1, 0))
        return matrix * own_col + other * cross_col, vectors

    scale_col = 1.0 / jnp.sqrt(cell_col[...])
    scale_row = 1.0 / jnp.sqrt(cell_row[...])
    tri = (
        unit * (low_row[...] + face_row[...] + screen_row[...])
        - (col == row + 1).astype(f32) * face_col[...]
        - ((col == row - 1) & (row < n)).astype(f32) * face_row[...]
    )
    matrix = scale_col * tri * scale_row
    whole = jnp.sum(matrix * matrix)

    def unsettled(state):
        sweep, off, _, _ = state
        return (sweep < 15) & (off > 1e-10 * whole)

    def one_sweep(state):
        sweep, _, matrix, vectors = state

        def two(_, held):
            held = stage(held[0], held[1], pairings[0])
            return stage(held[0], held[1], pairings[1])

        matrix, vectors = lax.fori_loop(0, n // 2, two, (matrix, vectors))
        rest = matrix * (1.0 - unit)
        return sweep + 1, jnp.sum(rest * rest), matrix, vectors

    _, _, _, vectors = lax.while_loop(
        unsettled, one_sweep, (jnp.int32(0), whole, matrix, unit)
    )
    modes = scale_col * vectors
    norm = jnp.sum(cell_col[...] * modes * modes, axis=0, keepdims=True)
    modes = modes * (1.0 / jnp.sqrt(jnp.where(lane < n, norm, 1.0)))
    rise = pltpu.roll(modes, n - 1, 0) - modes
    walls = jnp.where((row == 0) | (row == n - 1), 1.0, 0.0) * face_col[n - 1 : n, :]
    energy = (screen_col[...] + walls) * modes * modes
    energy = energy + jnp.where(row < n - 1, face_col[...], 0.0) * rise * rise
    values = jnp.sum(energy, axis=0, keepdims=True)
    total = jnp.sum(unit * values, axis=1, keepdims=True) + shift_row[...]
    ratio_ref[...] = 2.0 / (2.0 + total + jnp.sqrt(total * (total + 4.0)))

    size = ROWS * n

    def flags(shape, test):
        first = lax.broadcasted_iota(jnp.int32, shape, 0)
        second = lax.broadcasted_iota(jnp.int32, shape, 1)
        return jnp.where(test(first, second), 1.0, 0.0)

    pick_mode = flags((size, LANES), lambda a, b: a % n == b).astype(bf16)
    pick_layer = flags((size, n), lambda a, b: a // ROWS == b).astype(bf16)
    spread_layer = flags((n, size), lambda a, b: b // ROWS == a).astype(bf16)
    same_fore = flags((size, size), lambda a, b: a // n == b % ROWS)
    same_back = flags((size, size), lambda a, b: a % ROWS == b // n)
    across = (((1,), (1,)), ((), ()))
    for part, fore, back in zip(split(modes), (fore_high, fore_low), (back_high, back_low)):
        turned = lax.dot_general(pick_mode, part, across, preferred_element_type=f32)
        spread = jnp.dot(turned.astype(bf16), spread_layer, preferred_element_type=f32)
        fore[...] = (spread * same_fore).astype(bf16)
        layered = jnp.dot(pick_layer, part, preferred_element_type=f32)
        spread = lax.dot_general(
            layered.astype(bf16), pick_mode, across, preferred_element_type=f32
        )
        back[...] = (spread * same_back).astype(bf16)


def eigen(cell, face, screening, shift_row):
    n = cell.shape[0]
    size = ROWS * n

    def as_row(value):
        return jnp.pad(value, (0, LANES - n), constant_values=1.0)[None]

    table = jax.ShapeDtypeStruct((size, size), bf16)
    return pl.pallas_call(
        eigen_kernel,
        out_shape=(jax.ShapeDtypeStruct((n, shift_row.shape[1]), f32),) + (table,) * 4,
        compiler_params=pltpu.CompilerParams(vmem_limit_bytes=32 * 1024 * 1024),
        cost_estimate=cost(20_000_000_000, 4 * size * size),
        name="eigen",
    )(
        cell[:, None], as_row(cell), face[:, None], as_row(face), as_row(jnp.roll(face, 1)),
        screening[:, None], as_row(screening), shift_row,
    )


def forward_y_kernel(charge_ref, high_ref, low_ref, out_ref, rows_high, rows_low):
    @pl.when(pl.program_id(0) == 0)
    def _():
        high, low = split(charge_ref[...].reshape(rows_high.shape))
        rows_high[...] = high
        rows_low[...] = low

    result = product((rows_high[...], rows_low[...]), (high_ref[...], low_ref[...]))
    out_ref[...] = result.reshape(out_ref.shape)


def forward_y(charge, chunk, high, low, slabs):
    depth, x_local, width = charge.shape
    rows = x_local // CHUNKS
    part = width // slabs
    return pl.pallas_call(
        forward_y_kernel,
        out_shape=jax.ShapeDtypeStruct((slabs, depth, rows, part), f32),
        grid=(slabs,),
        in_specs=[
            pl.BlockSpec((depth, rows, width), lambda i: (0, chunk, 0)),
            pl.BlockSpec((width, part), lambda i: (0, i)),
            pl.BlockSpec((width, part), lambda i: (0, i)),
        ],
        out_specs=pl.BlockSpec((1, depth, rows, part), lambda i: (i, 0, 0, 0)),
        scratch_shapes=[pltpu.VMEM((depth * rows, width), bf16)] * 2,
        compiler_params=params(),
        cost_estimate=cost(6 * depth * rows * width * width, 4 * width * width),
        name="forward_y",
    )(charge, high, low)


def rise_kernel(first, value_ref, high_ref, low_ref, ratio_ref, *rest):
    if first:
        out_ref, ends_ref, power_ref = rest
    else:
        ends_in, power_in, out_ref, ends_ref, power_ref = rest
    layers, _, part = value_ref.shape

    @pl.when(pl.program_id(0) == 0)
    def _():
        if first:
            ends_ref[...] = jnp.zeros_like(ends_ref)
            power_ref[...] = ratio_ref[...]
        else:
            ends_ref[...] = ends_in[...]
            power_ref[...] = power_in[...]

    ratio = ratio_ref[...]
    for start in range(0, STEP, ROWS):
        block = value_ref[:, start : start + ROWS, :].reshape(layers * ROWS, part)
        modes = product((high_ref[...], low_ref[...]), split(block))
        value, total, power = ends_ref[0], ends_ref[1], power_ref[...]
        for x in range(ROWS):
            value = modes[x * layers : (x + 1) * layers] + ratio * value
            out_ref[start + x] = value
            total = total + power * value
            power = power * ratio
        ends_ref[0] = value
        ends_ref[1] = total
        power_ref[...] = power


def rise(value, high, low, ratio, state):
    layers, rows, part = value.shape
    table = pl.BlockSpec(high.shape, lambda i: (0, 0))
    plane = pl.BlockSpec((layers, part), lambda i: (0, 0))
    pair = pl.BlockSpec((2, layers, part), lambda i: (0, 0, 0))
    return pl.pallas_call(
        functools.partial(rise_kernel, state is None),
        out_shape=(
            jax.ShapeDtypeStruct((rows, layers, part), f32),
            jax.ShapeDtypeStruct((2, layers, part), f32),
            jax.ShapeDtypeStruct((layers, part), f32),
        ),
        grid=(rows // STEP,),
        in_specs=[pl.BlockSpec((layers, STEP, part), lambda i: (0, i, 0)), table, table, plane]
        + ([] if state is None else [pair, plane]),
        out_specs=(pl.BlockSpec((STEP, layers, part), lambda i: (i, 0, 0)), pair, plane),
        compiler_params=params(),
        cost_estimate=cost(6 * ROWS * layers * layers * rows * part, 8 * rows * layers * part),
        name="rise",
    )(value, high, low, ratio, *(() if state is None else state))


def link_kernel(x_local, place_ref, ratio_ref, ends_ref, enter_ref, leave_ref):
    blocks = ends_ref.shape[0]
    place = place_ref[0]
    ratio = ratio_ref[...]

    def raised(base, count):
        value = None
        while count:
            if count & 1:
                value = base if value is None else value * base
            base = base * base
            count >>= 1
        return value

    across = raised(ratio, x_local)
    around = 1.0 / (1.0 - raised(across, blocks))
    both = ratio * ratio * (1.0 - across * across) / ((1.0 - ratio) * (1.0 + ratio))
    last = ends_ref[0, 0]
    for block in range(1, blocks):
        last = ends_ref[block, 0] + across * last
    last = last * around
    tops = []
    enter = jnp.zeros_like(last)
    for block in range(blocks):
        enter = jnp.where(place == block, last, enter)
        tops.append(ends_ref[block, 1] + both * last)
        last = ends_ref[block, 0] + across * last
    enter_ref[...] = enter
    first = tops[-1]
    for block in reversed(range(blocks - 1)):
        first = tops[block] + across * first
    first = first * around
    leave = jnp.zeros_like(first)
    for block in reversed(range(blocks)):
        leave = jnp.where(place == block, first, leave)
        first = tops[block] + across * first
    leave_ref[...] = leave


def link(place, ratio, gathered, x_local):
    plane = jax.ShapeDtypeStruct(ratio.shape, f32)
    vmem = pl.BlockSpec(memory_space=pltpu.VMEM)
    return pl.pallas_call(
        functools.partial(link_kernel, x_local),
        out_shape=(plane, plane),
        in_specs=[pl.BlockSpec(memory_space=pltpu.SMEM), vmem, vmem],
        out_specs=(vmem, vmem),
        cost_estimate=cost(10 * gathered.size, 4 * gathered.size),
        name="link",
    )(place, ratio, gathered)


def fall_kernel(
    first_row, value_ref, high_ref, low_ref, ratio_ref, enter_ref, leave_ref,
    out_ref, carry_ref, near_ref, far_ref, held_ref,
):
    layers, _, part = out_ref.shape
    ratio = ratio_ref[...]

    @pl.when(pl.program_id(0) == 0)
    def _():
        carry_ref[...] = leave_ref[...]
        power = ratio
        for x in range(ROWS):
            near_ref[x] = power
            if x < ROWS - 1:
                power = power * ratio
        value = enter_ref[...]
        for block in range(far_ref.shape[0]):
            far_ref[block] = value
            value = value * power

    step = pl.num_programs(0) - 1 - pl.program_id(0)
    value = carry_ref[...]
    for start in reversed(range(0, STEP, ROWS)):
        far = far_ref[(first_row + start) // ROWS + step * (STEP // ROWS)]
        for x in reversed(range(ROWS)):
            value = ratio * (value_ref[start + x] + near_ref[x] * far + value)
            held_ref[x * layers : (x + 1) * layers] = value
        solved = product((high_ref[...], low_ref[...]), split(held_ref[...]))
        out_ref[:, start : start + ROWS, :] = solved.reshape(layers, ROWS, part)
    carry_ref[...] = value


def fall(value, chunk, x_local, high, low, ratio, enter, leave):
    rows, layers, part = value.shape
    steps = rows // STEP
    table = pl.BlockSpec(high.shape, lambda i: (0, 0))
    plane = pl.BlockSpec((layers, part), lambda i: (0, 0))
    return pl.pallas_call(
        functools.partial(fall_kernel, chunk * rows),
        out_shape=(
            jax.ShapeDtypeStruct((layers, rows, part), f32),
            jax.ShapeDtypeStruct((layers, part), f32),
        ),
        grid=(steps,),
        in_specs=[
            pl.BlockSpec((STEP, layers, part), lambda i: (steps - 1 - i, 0, 0)),
            table, table, plane, plane, plane,
        ],
        out_specs=(
            pl.BlockSpec((layers, STEP, part), lambda i: (0, steps - 1 - i, 0)),
            plane,
        ),
        scratch_shapes=[
            pltpu.VMEM((ROWS, layers, part), f32),
            pltpu.VMEM((x_local // ROWS, layers, part), f32),
            pltpu.VMEM((ROWS * layers, part), f32),
        ],
        compiler_params=params(),
        cost_estimate=cost(6 * ROWS * layers * layers * rows * part, 8 * rows * layers * part),
        name="fall",
    )(value, high, low, ratio, enter, leave)


def back_y_kernel(value_ref, high_ref, low_ref, *rest):
    out_ref, rows_high, rows_low = rest[-3:]
    slabs, depth, rows, part = value_ref.shape

    @pl.when(pl.program_id(0) == 0)
    def _():
        for slab in range(slabs):
            high, low = split(value_ref[slab].reshape(depth * rows, part))
            rows_high[:, slab * part : (slab + 1) * part] = high
            rows_low[:, slab * part : (slab + 1) * part] = low

    result = product((rows_high[...], rows_low[...]), (high_ref[...], low_ref[...]))
    out_ref[...] = result.reshape(out_ref.shape)


def back_y(value, chunk, x_local, high, low, held):
    _, depth, rows, _ = value.shape
    width = high.shape[0]
    columns = min(256, width)
    operands = [value, high, low]
    in_specs = [
        pl.BlockSpec(value.shape, lambda i: (0, 0, 0, 0)),
        pl.BlockSpec((width, columns), lambda i: (0, i)),
        pl.BlockSpec((width, columns), lambda i: (0, i)),
    ]
    aliases = {}
    if held is not None:
        operands.append(held)
        in_specs.append(pl.BlockSpec(memory_space=pl.ANY))
        aliases = {3: 0}
    return pl.pallas_call(
        back_y_kernel,
        out_shape=jax.ShapeDtypeStruct((depth, x_local, width), f32),
        grid=(width // columns,),
        in_specs=in_specs,
        out_specs=pl.BlockSpec((depth, rows, columns), lambda i: (0, chunk, i)),
        scratch_shapes=[pltpu.VMEM((depth * rows, width), bf16)] * 2,
        input_output_aliases=aliases,
        compiler_params=params(),
        cost_estimate=cost(6 * depth * rows * width * width, 4 * width * width),
        name="back_y",
    )(*operands)


def body(charge, cell_permittivity, face_permittivity, screening):
    depth, x_local, width = charge.shape
    slabs = lax.axis_size("gz")
    layers = depth * slabs
    rows = x_local // CHUNKS
    part = width // slabs
    table = basis_table(width)
    fore_high, fore_low = halves(table * mode_weights(width)[None, :])
    back_high, back_low = halves(np.ascontiguousarray(table.T))
    shift_row = lax.dynamic_slice_in_dim(
        jnp.asarray(mode_shift(width)[None]), lax.axis_index("gz") * part, part, 1
    )
    place = lax.axis_index("gx").astype(jnp.int32).reshape(1)
    exchange = functools.partial(
        lax.all_to_all, axis_name="gz", split_axis=0, concat_axis=0, tiled=True
    )
    ratio, to_high, to_low, from_high, from_low = eigen(
        cell_permittivity, face_permittivity, screening, shift_row
    )
    state = None
    risen = []
    for chunk in range(CHUNKS):
        sent = forward_y(charge, chunk, fore_high, fore_low, slabs)
        got = exchange(sent).reshape(layers, rows, part)
        value, *state = rise(got, to_high, to_low, ratio, state)
        risen.append(value)
    gathered = lax.all_gather(state[0], "gx", axis=0)
    enter, leave = link(place, ratio, gathered, x_local)
    result = None
    for chunk in reversed(range(CHUNKS)):
        sent, leave = fall(
            risen[chunk], chunk, x_local, from_high, from_low, ratio, enter, leave
        )
        got = exchange(sent.reshape(slabs, depth, rows, part))
        result = back_y(got, chunk, x_local, back_high, back_low, result)
    return result


def solution(mesh):
    in_specs = (P("gz", "gx", None), P(), P(), P())
    out_specs = P("gz", "gx", None)
    return jax.shard_map(body, mesh=mesh, in_specs=in_specs, out_specs=out_specs, check_vma=False)
```

profile of v0, /device:TPU:1, one launch (start us, length us, event | category | flops | bytes accessed | tf_op | source)
XLA Modules:
  0.0 261.2 jit_solution(11656527748321006744)
XLA Ops:
  0.0 1.6 copy-done.14
  1.6 6.3 %forward_y.2 = f32[4,8,64,256]{3,2,1,0:T(8,128)S(1)} custom-call(f32[8,128,1024]{2,1,0:T(8,128)} %charge_ref.3, bf16[1024,1024]{1,0:T(8,128)(2,1)S(1)} %copy-done.14, bf16[1024,1024]{1,0:T(8,128)(2,1)} %constant.28.clone.low_ref), custom_call_target="tpu_custom_call" | custom-call | flops 3221225472 | bytes 4194304 | tf_op jit(solution)/shard_map/forward_y/pallas_call | solution.py:221
  9.3 4.4 %all-to-all-start = ((f32[4,8,64,256]{3,2,1,0:T(8,128)}), f32[4,8,64,256]{3,2,1,0:T(8,128)S(1)}, u32[]{:S(2)}, u32[]{:S(2)}) async-start(f32[4,8,64,256]{3,2,1,0:T(8,128)} %copy-done.2), calls=%async_computation | async-start | bytes 4194304 | tf_op jit(solution)/shard_map/all_to_all | solution.py:473
  16.0 1.6 copy-done.15
  17.6 6.3 %forward_y.3 = f32[4,8,64,256]{3,2,1,0:T(8,128)S(1)} custom-call(f32[8,128,1024]{2,1,0:T(8,128)} %charge_ref.3, bf16[1024,1024]{1,0:T(8,128)(2,1)S(1)} %copy-done.15, bf16[1024,1024]{1,0:T(8,128)(2,1)} %constant.28.clone.low_ref), custom_call_target="tpu_custom_call" | custom-call | flops 3221225472 | bytes 4194304 | tf_op jit(solution)/shard_map/forward_y/pallas_call | solution.py:221
  25.3 12.9 %all-to-all-done = f32[4,8,64,256]{3,2,1,0:T(8,128)S(1)} async-done(((f32[4,8,64,256]{3,2,1,0:T(8,128)}), f32[4,8,64,256]{3,2,1,0:T(8,128)S(1)}, u32[]{:S(2)}, u32[]{:S(2)}) %all-to-all-start) | async-done | bytes 2097184 | tf_op jit(solution)/shard_map/all_to_all | solution.py:473
  38.1 5.6 %all-to-all-start.1 = ((f32[4,8,64,256]{3,2,1,0:T(8,128)}), f32[4,8,64,256]{3,2,1,0:T(8,128)}, u32[]{:S(2)}, u32[]{:S(2)}) async-start(f32[4,8,64,256]{3,2,1,0:T(8,128)} %copy-done.3), calls=%async_computation.1 | async-start | bytes 4194304 | tf_op jit(solution)/shard_map/all_to_all | solution.py:473
  43.8 101.0 %eigen.1 = (f32[32,256]{1,0:T(8,128)S(1)}, bf16[256,256]{1,0:T(8,128)(2,1)S(1)}, bf16[256,256]{1,0:T(8,128)(2,1)S(1)}, bf16[256,256]{1,0:T(8,128)(2,1)S(1)}, bf16[256,256]{1,0:T(8,128)(2,1)S(1)}) custom-call(f32[32,1]{1,0:T(8,128)S(1)} %copy.14.cell_col, f32[1,128]{1,0:T(1,128)S(1)} %get-tuple-element.37.cell_row, f32[32,1]{1,0:T(8,128)S(1)} %copy.15.face_col, ...), custom_call_target="tpu_custom_call" | custom-call | flops 20000000000 | bytes 262144 | tf_op jit(solution)/shard_map/eigen/pallas_call | solution.py:194
  144.7 1.9 rise.2
  148.0 4.0 %rise.3 = (f32[64,32,256]{2,1,0:T(8,128)S(1)}, f32[2,32,256]{2,1,0:T(8,128)S(1)}, f32[32,256]{1,0:T(8,128)}) custom-call(f32[32,64,256]{2,1,0:T(8,128)} %bitcast.9.value_ref, bf16[256,256]{1,0:T(8,128)(2,1)S(1)} %get-tuple-element.20.high_ref, bf16[256,256]{1,0:T(8,128)(2,1)S(1)} %get-tuple-element.21.low_ref, f32[32,256]{1,0:T(8,128)S(1)} %get-tuple-element.22.ratio_ref, ...), custom_call_target="tpu_custom_call" | custom-call | flops 805306368 | bytes 4194304 | tf_op jit(solution)/shard_map/rise/pallas_call | solution.py:274
  151.9 28.4 %all-gather = f32[16,32,256]{2,1,0:T(8,128)} all-gather(f32[2,32,256]{2,1,0:T(8,128)S(1)} %get-tuple-element.28), channel_id=2, replica_groups=mesh['gx'=8,'gz'=4] {'gx'}, dimensions={0}, use_global_device_ids=true | all-gather | bytes 589824 | tf_op jit(solution)/shard_map/all_gather | solution.py:476
  180.4 1.8 link.1
  184.5 2.0 fall.2
  187.8 9.8 %all-to-all-start.3 = ((f32[4,8,64,256]{3,2,1,0:T(8,128)}), f32[4,8,64,256]{3,2,1,0:T(8,128)S(1)}, u32[]{:S(2)}, u32[]{:S(2)}) async-start(f32[4,8,64,256]{3,2,1,0:T(8,128)} %bitcast.20), calls=%async_computation.3 | async-start | bytes 4194304 | tf_op jit(solution)/shard_map/all_to_all | solution.py:483
  197.5 1.6 copy-done.17
  199.1 2.6 fall.3
  203.0 19.2 %all-to-all-done.3.value_ref = f32[4,8,64,256]{3,2,1,0:T(8,128)S(1)} async-done(((f32[4,8,64,256]{3,2,1,0:T(8,128)}), f32[4,8,64,256]{3,2,1,0:T(8,128)S(1)}, u32[]{:S(2)}, u32[]{:S(2)}) %all-to-all-start.3) | async-done | bytes 2097184 | tf_op jit(solution)/shard_map/all_to_all | solution.py:483
  223.5 4.6 %all-to-all-start.2 = ((f32[4,8,64,256]{3,2,1,0:T(8,128)}), f32[4,8,64,256]{3,2,1,0:T(8,128)S(1)}, u32[]{:S(2)}, u32[]{:S(2)}) async-start(f32[4,8,64,256]{3,2,1,0:T(8,128)} %bitcast.19), calls=%async_computation.2 | async-start | bytes 4194304 | tf_op jit(solution)/shard_map/all_to_all | solution.py:483
  228.1 1.6 copy-done
  229.7 1.6 copy-done.5
  231.3 6.6 %back_y.2.rest_0_ = f32[8,128,1024]{2,1,0:T(8,128)} custom-call(f32[4,8,64,256]{3,2,1,0:T(8,128)S(1)} %copy-done.5, bf16[1024,1024]{1,0:T(8,128)(2,1)S(1)} %copy-done, bf16[1024,1024]{1,0:T(8,128)(2,1)} %constant.30.clone.low_ref), custom_call_target="tpu_custom_call" | custom-call | flops 3221225472 | bytes 4194304 | tf_op jit(solution)/shard_map/back_y/pallas_call | solution.py:436
  237.9 15.0 %all-to-all-done.2.value_ref = f32[4,8,64,256]{3,2,1,0:T(8,128)S(1)} async-done(((f32[4,8,64,256]{3,2,1,0:T(8,128)}), f32[4,8,64,256]{3,2,1,0:T(8,128)S(1)}, u32[]{:S(2)}, u32[]{:S(2)}) %all-to-all-start.2) | async-done | bytes 2097184 | tf_op jit(solution)/shard_map/all_to_all | solution.py:483
  253.0 1.6 copy-done.1
  254.6 6.6 %back_y.3 = f32[8,128,1024]{2,1,0:T(8,128)} custom-call(f32[4,8,64,256]{3,2,1,0:T(8,128)S(1)} %all-to-all-done.2.value_ref, bf16[1024,1024]{1,0:T(8,128)(2,1)S(1)} %copy-done.1, bf16[1024,1024]{1,0:T(8,128)(2,1)} %constant.30.clone.low_ref, f32[8,128,1024]{2,1,0:T(8,128)} %back_y.2.rest_0_), custom_call_target="tpu_custom_call", output_to_operand_aliasing={{}: (3, {})} | custom-call | flops 3221225472 | bytes 4194304 | tf_op jit(solution)/shard_map/back_y/pallas_call | solution.py:436
  (44 shorter events, 12.6 us)
Async XLA Ops:
  0.0 1.6 copy-start.14
  7.9 1.3 copy-start.2
  9.3 4.4 %copy-start.18 = (f32[32]{0:T(128)S(1)}, f32[32]{0:T(128)}, u32[]{:S(2)}) copy-start(f32[32]{0:T(128)} %param.11) | copy-start | bytes 388
  9.3 5.1 %copy-start.20 = (f32[32]{0:T(128)S(1)}, f32[32]{0:T(128)}, u32[]{:S(2)}) copy-start(f32[32]{0:T(128)} %param.12) | copy-start | bytes 388
  9.3 5.2 %copy-start.19 = (f32[32]{0:T(128)S(1)}, f32[32]{0:T(128)}, u32[]{:S(2)}) copy-start(f32[32]{0:T(128)} %param.10) | copy-start | bytes 388
  9.3 28.9 %all-to-all-start = ((f32[4,8,64,256]{3,2,1,0:T(8,128)}), f32[4,8,64,256]{3,2,1,0:T(8,128)S(1)}, u32[]{:S(2)}, u32[]{:S(2)}) async-start(f32[4,8,64,256]{3,2,1,0:T(8,128)} %copy-done.2), calls=%async_computation | async-start | bytes 4194304 | tf_op jit(solution)/shard_map/all_to_all | solution.py:473
  16.0 1.6 copy-start.15
  23.9 1.3 copy-start.3
  38.1 109.8 %all-to-all-start.1 = ((f32[4,8,64,256]{3,2,1,0:T(8,128)}), f32[4,8,64,256]{3,2,1,0:T(8,128)}, u32[]{:S(2)}, u32[]{:S(2)}) async-start(f32[4,8,64,256]{3,2,1,0:T(8,128)} %copy-done.3), calls=%async_computation.1 | async-start | bytes 4194304 | tf_op jit(solution)/shard_map/all_to_all | solution.py:473
  144.7 7.2 %copy-start.8 = (f32[32,256]{1,0:T(8,128)}, f32[32,256]{1,0:T(8,128)S(1)}, u32[]{:S(2)}) copy-start(f32[32,256]{1,0:T(8,128)S(1)} %get-tuple-element.22.ratio_ref) | copy-start | bytes 98308
  146.6 1.3 copy-start.16
  182.2 0.8 copy-start.9
  182.9 0.8 copy-start.11
  186.4 1.3 copy-start.7
  187.8 9.8 %copy-start.10 = (f32[32,256]{1,0:T(8,128)S(1)}, f32[32,256]{1,0:T(8,128)}, u32[]{:S(2)}) copy-start(f32[32,256]{1,0:T(8,128)} %copy-done.8) | copy-start | bytes 98308
  187.8 9.8 %copy-start.12 = (f32[32,256]{1,0:T(8,128)S(1)}, f32[32,256]{1,0:T(8,128)}, u32[]{:S(2)}) copy-start(f32[32,256]{1,0:T(8,128)} %get-tuple-element.29.enter_ref) | copy-start | bytes 98308
  187.8 34.5 %all-to-all-start.3 = ((f32[4,8,64,256]{3,2,1,0:T(8,128)}), f32[4,8,64,256]{3,2,1,0:T(8,128)S(1)}, u32[]{:S(2)}, u32[]{:S(2)}) async-start(f32[4,8,64,256]{3,2,1,0:T(8,128)} %bitcast.20), calls=%async_computation.3 | async-start | bytes 4194304 | tf_op jit(solution)/shard_map/all_to_all | solution.py:483
  197.5 1.6 copy-start.17
  201.7 1.3 copy-start.6
  222.2 1.3 copy-start.4
  223.5 29.4 %all-to-all-start.2 = ((f32[4,8,64,256]{3,2,1,0:T(8,128)}), f32[4,8,64,256]{3,2,1,0:T(8,128)S(1)}, u32[]{:S(2)}, u32[]{:S(2)}) async-start(f32[4,8,64,256]{3,2,1,0:T(8,128)} %bitcast.19), calls=%async_computation.2 | async-start | bytes 4194304 | tf_op jit(solution)/shard_map/all_to_all | solution.py:483
  228.1 1.6 copy-start
  229.7 1.6 copy-start.5
  253.0 1.6 copy-start.1
  (1 other events, 0.8 us)
where the time goes:
time: 263 us; the launch traced here: 261 us
  Pallas kernels  139 us (53%)
  waiting for transfers between devices  47.1 us (18%)
  blocking collectives  28.4 us (11%)
  starting transfers between devices  24.3 us (9%)
  local copies, waits for them, and re-layouts  21.3 us (8%)
    pallas_call x1, Pallas kernels, eigen(): pl.pallas_call(eigen_kernel, out_shape=(jax.ShapeDtypeStruct((n, shift_ro...  101 us
    all_to_all x2, waiting for transfers between devices, body(): got = exchange(sent.reshape(slabs, depth, rows, part))  34.2 us
    all_gather x1, blocking collectives, body(): gathered = lax.all_gather(state[0], 'gx', axis=0)  28.4 us
    unnamed x42, local copies, waits for them, and re-layouts  19.8 us
    all_to_all x2, starting transfers between devices, body(): got = exchange(sent.reshape(slabs, depth, rows, part))  14.3 us
    pallas_call x2, Pallas kernels, back_y(): pl.pallas_call(back_y_kernel, out_shape=jax.ShapeDtypeStruct((depth, x_lo...  13.2 us
    all_to_all x2, waiting for transfers between devices, body(): got = exchange(sent).reshape(layers, rows, part)  12.9 us
    pallas_call x2, Pallas kernels, forward_y(): pl.pallas_call(forward_y_kernel, out_shape=jax.ShapeDtypeStruct((slabs, d...  12.7 us
  transfers between devices with their start and end apart: 4, of which 3 were waited for; matrix products, arithmetic and copies ran while one was open for 1% of the time, Pallas kernels for 45%

commit v1 on v0

--- a/solution.py
+++ b/solution.py
@@ -12,6 +12,8 @@
 f32 = jnp.float32
 bf16 = jnp.bfloat16
 LANES = 128
+VMEM = 60 * 1024 * 1024
+MESH = pl.DeviceIdType.MESH
 ROWS = 8
 STEP = 16
 CHUNKS = 2
@@ -19,7 +21,7 @@
 
 def params():
     return pltpu.CompilerParams(
-        vmem_limit_bytes=48 * 1024 * 1024, dimension_semantics=("arbitrary",)
+        vmem_limit_bytes=VMEM, dimension_semantics=("arbitrary",)
     )
 
 
@@ -68,15 +70,43 @@
     return dot(left[0], right[0]) + (dot(left[0], right[1]) + dot(left[1], right[0]))
 
 
-def eigen_kernel(
-    cell_col, cell_row, face_col, face_row, low_row, screen_col, screen_row, shift_row,
-    ratio_ref, fore_high, fore_low, back_high, back_low,
-):
-    n = cell_col.shape[0]
+def one_stage(held, pair):
+    n = held.shape[0]
+    unit, mate, low_cols, low_rows, paired_cols, paired_rows = pair
+
+    def lane_mates(value):
+        return jnp.where(low_cols, pltpu.roll(value, LANES - 1, 1), pltpu.roll(value, 1, 1))
+
+    def row_mates(value):
+        return jnp.where(low_rows, pltpu.roll(value, n - 1, 0), pltpu.roll(value, 1, 0))
+
+    def rotation(other, axis, low, paired):
+        gap = jnp.sum(mate * other - unit * held, axis=axis, keepdims=True)
+        twice = jnp.sum(mate * held + unit * other, axis=axis, keepdims=True)
+        square = jnp.maximum(gap * gap + twice * twice, 1e-35)
+        inverse = lax.rsqrt(square)
+        inverse = inverse * (1.5 - 0.5 * square * inverse * inverse)
+        half = 0.5 + 0.5 * jnp.abs(gap) * inverse
+        root = lax.rsqrt(half)
+        root = root * (1.5 - 0.5 * half * root * root)
+        positive = (gap > 0.0) | ((gap == 0.0) & low)
+        sine = 0.5 * jnp.where(positive, twice, -twice) * inverse * root
+        return jnp.where(paired, sine, 1.0), jnp.where(paired, half * root, 0.0)
+
+    by_lane = lane_mates(held)
+    by_row = row_mates(held)
+    by_both = row_mates(by_lane)
+    own_row, cross_row = rotation(by_lane, 0, low_cols[:1], paired_cols[:1])
+    own_col, cross_col = rotation(by_row, 1, low_rows[:, :1], paired_rows[:, :1])
+    return own_col * (own_row * held + cross_row * by_lane) + cross_col * (
+        own_row * by_row + cross_row * by_both
+    )
+
+
+def pairings(n):
     shape = (n, LANES)
     row = lax.broadcasted_iota(jnp.int32, shape, 0)
     col = lax.broadcasted_iota(jnp.int32, shape, 1)
-    lane = lax.broadcasted_iota(jnp.int32, (1, LANES), 1)
     unit = (row == col).astype(f32)
 
     def pairing(parity):
@@ -88,75 +118,78 @@
 
         mate = jnp.where(lower(col), col + 1, jnp.where(upper(col), col - 1, -1))
         return (
+            unit,
             (row == mate).astype(f32),
             lower(col),
             lower(row),
-            lower(lane),
-            lower(lane) | upper(lane),
+            lower(col) | upper(col),
+            lower(row) | upper(row),
         )
 
-    pairings = (pairing(0), pairing(1))
-
-    def lane_mates(value, low):
-        return jnp.where(low, pltpu.roll(value, LANES - 1, 1), pltpu.roll(value, 1, 1))
-
-    def stage(matrix, vectors, pair):
-        mate, low_cols, low_rows, low_lane, paired = pair
-        other = lane_mates(matrix, low_cols)
-        gap = jnp.sum(mate * other - unit * matrix, axis=0, keepdims=True)
-        twice = jnp.sum(mate * matrix + unit * other, axis=0, keepdims=True)
-        positive = (gap > 0.0) | ((gap == 0.0) & low_lane)
-        size = jnp.abs(gap) + jnp.sqrt(gap * gap + twice * twice) + 1e-30
-        tangent = jnp.where(positive, twice, -twice) / size
-        square = 1.0 + tangent * tangent
-        cosine = lax.rsqrt(square)
-        cosine = cosine * (1.5 - 0.5 * square * cosine * cosine)
-        own = jnp.where(paired, cosine * tangent, 1.0)
-        cross = jnp.where(paired, cosine, 0.0)
-        own_col = jnp.sum(unit * own, axis=1, keepdims=True)
-        cross_col = jnp.sum(unit * cross, axis=1, keepdims=True)
-        vectors = vectors * own + lane_mates(vectors, low_cols) * cross
-        matrix = matrix * own + other * cross
-        other = jnp.where(low_rows, pltpu.roll(matrix, n - 1, 0), pltpu.roll(matrix, 1, 0))
-        return matrix * own_col + other * cross_col, vectors
-
-    scale_col = 1.0 / jnp.sqrt(cell_col[...])
-    scale_row = 1.0 / jnp.sqrt(cell_row[...])
+    return pairing(0), pairing(1)
+
+
+def one_sweep(held, pairs):
+    def two(_, value):
+        return one_stage(one_stage(value, pairs[0]), pairs[1])
+
+    return lax.fori_loop(0, held.shape[0] // 2, two, held)
+
+
+def begin_kernel(
+    sweeps, cell_col, cell_row, face_col, face_row, low_row, screen_row, after_ref, held_ref
+):
+    n = cell_col.shape[0]
+    row = lax.broadcasted_iota(jnp.int32, held_ref.shape, 0)
+    col = lax.broadcasted_iota(jnp.int32, held_ref.shape, 1)
     tri = (
-        unit * (low_row[...] + face_row[...] + screen_row[...])
+        (row == col).astype(f32) * (low_row[...] + face_row[...] + screen_row[...])
         - (col == row + 1).astype(f32) * face_col[...]
-        - ((col == row - 1) & (row < n)).astype(f32) * face_row[...]
-    )
-    matrix = scale_col * tri * scale_row
-    whole = jnp.sum(matrix * matrix)
+        - (col == row - 1).astype(f32) * face_row[...]
+    )
+    matrix = tri * (1.0 / jnp.sqrt(cell_col[...])) * (1.0 / jnp.sqrt(cell_row[...]))
+    held = jnp.where(col < n, matrix, (col == row + n).astype(f32))
+    pairs = pairings(n)
+    held_ref[...] = lax.fori_loop(0, sweeps, lambda _, value: one_sweep(value, pairs), held)
+
+
+def end_kernel(
+    held_ref, cell_row, face_row, screen_row, shift_row, after_ref,
+    ratio_ref, fore_high, fore_low, back_high, back_low,
+):
+    n = held_ref.shape[0]
+    row = lax.broadcasted_iota(jnp.int32, held_ref.shape, 0)
+    col = lax.broadcasted_iota(jnp.int32, held_ref.shape, 1)
+    diagonal = row == col
+    beside = (col < n) & (row != col)
+    pairs = pairings(n)
 
     def unsettled(state):
-        sweep, off, _, _ = state
+        sweep, off, whole, _ = state
         return (sweep < 15) & (off > 1e-10 * whole)
 
-    def one_sweep(state):
-        sweep, _, matrix, vectors = state
-
-        def two(_, held):
-            held = stage(held[0], held[1], pairings[0])
-            return stage(held[0], held[1], pairings[1])
-
-        matrix, vectors = lax.fori_loop(0, n // 2, two, (matrix, vectors))
-        rest = matrix * (1.0 - unit)
-        return sweep + 1, jnp.sum(rest * rest), matrix, vectors
-
-    _, _, _, vectors = lax.while_loop(
-        unsettled, one_sweep, (jnp.int32(0), whole, matrix, unit)
-    )
-    modes = scale_col * vectors
-    norm = jnp.sum(cell_col[...] * modes * modes, axis=0, keepdims=True)
-    modes = modes * (1.0 / jnp.sqrt(jnp.where(lane < n, norm, 1.0)))
-    rise = pltpu.roll(modes, n - 1, 0) - modes
-    walls = jnp.where((row == 0) | (row == n - 1), 1.0, 0.0) * face_col[n - 1 : n, :]
-    energy = (screen_col[...] + walls) * modes * modes
-    energy = energy + jnp.where(row < n - 1, face_col[...], 0.0) * rise * rise
-    values = jnp.sum(energy, axis=0, keepdims=True)
-    total = jnp.sum(unit * values, axis=1, keepdims=True) + shift_row[...]
+    def sweep_on(state):
+        sweep, _, _, held = state
+        held = one_sweep(held, pairs)
+        return sweep + 1, *sizes(held), held
+
+    def sizes(held):
+        square = held * held
+        return jnp.sum(jnp.where(beside, square, 0.0)), jnp.sum(jnp.where(diagonal, square, 0.0))
+
+    held = held_ref[...]
+    held = lax.while_loop(unsettled, sweep_on, (jnp.int32(0), *sizes(held), held))[3]
+    layer = col < n
+    modes = jnp.where(layer, pltpu.roll(held, LANES - n, 1), 0.0) / jnp.sqrt(cell_row[...])
+    norm = jnp.sum(cell_row[...] * modes * modes, axis=1, keepdims=True)
+    modes = modes * (1.0 / jnp.sqrt(norm))
+    slope = pltpu.roll(modes, LANES - 1, 1) - modes
+    wall = face_row[:, n - 1 : n]
+    walls = jnp.where((col == 0) | (col == n - 1), 1.0, 0.0) * wall
+    energy = (screen_row[...] + walls) * modes * modes
+    energy = energy + jnp.where(col < n - 1, face_row[...], 0.0) * slope * slope
+    values = jnp.sum(energy, axis=1, keepdims=True)
+    total = values + shift_row[...]
     ratio_ref[...] = 2.0 / (2.0 + total + jnp.sqrt(total * (total + 4.0)))
 
     size = ROWS * n
@@ -166,44 +199,60 @@
         second = lax.broadcasted_iota(jnp.int32, shape, 1)
         return jnp.where(test(first, second), 1.0, 0.0)
 
-    pick_mode = flags((size, LANES), lambda a, b: a % n == b).astype(bf16)
-    pick_layer = flags((size, n), lambda a, b: a // ROWS == b).astype(bf16)
-    spread_layer = flags((n, size), lambda a, b: b // ROWS == a).astype(bf16)
+    pick_mode = flags((size, n), lambda a, b: a % n == b).astype(bf16)
+    spread_mode = flags((n, size), lambda a, b: b % n == a).astype(bf16)
+    pick_layer = flags((size, LANES), lambda a, b: a // ROWS == b).astype(bf16)
+    spread_layer = flags((LANES, size), lambda a, b: b // ROWS == a).astype(bf16)
     same_fore = flags((size, size), lambda a, b: a // n == b % ROWS)
     same_back = flags((size, size), lambda a, b: a % ROWS == b // n)
     across = (((1,), (1,)), ((), ()))
     for part, fore, back in zip(split(modes), (fore_high, fore_low), (back_high, back_low)):
-        turned = lax.dot_general(pick_mode, part, across, preferred_element_type=f32)
+        turned = jnp.dot(pick_mode, part, preferred_element_type=f32)
         spread = jnp.dot(turned.astype(bf16), spread_layer, preferred_element_type=f32)
         fore[...] = (spread * same_fore).astype(bf16)
-        layered = jnp.dot(pick_layer, part, preferred_element_type=f32)
-        spread = lax.dot_general(
-            layered.astype(bf16), pick_mode, across, preferred_element_type=f32
-        )
+        layered = lax.dot_general(pick_layer, part, across, preferred_element_type=f32)
+        spread = jnp.dot(layered.astype(bf16), spread_mode, preferred_element_type=f32)
         back[...] = (spread * same_back).astype(bf16)
 
 
-def eigen(cell, face, screening, shift_row):
+def as_row(value):
+    return jnp.pad(value, (0, LANES - value.shape[0]), constant_values=1.0)[None]
+
+
+def eigen_begin(cell, face, screening, after):
+    n = cell.shape[0]
+    vmem = pl.BlockSpec(memory_space=pltpu.VMEM)
+    return pl.pallas_call(
+        functools.partial(begin_kernel, 2),
+        out_shape=jax.ShapeDtypeStruct((n, LANES), f32),
+        in_specs=[vmem] * 6 + [pl.BlockSpec(memory_space=pl.ANY)],
+        out_specs=vmem,
+        compiler_params=pltpu.CompilerParams(vmem_limit_bytes=VMEM),
+        cost_estimate=cost(10_000_000_000, 4 * n * LANES),
+        name="eigen_begin",
+    )(
+        cell[:, None], as_row(cell), face[:, None], as_row(face), as_row(jnp.roll(face, 1)),
+        as_row(screening), after,
+    )
+
+
+def eigen_end(held, cell, face, screening, shift_row, after):
     n = cell.shape[0]
     size = ROWS * n
-
-    def as_row(value):
-        return jnp.pad(value, (0, LANES - n), constant_values=1.0)[None]
-
     table = jax.ShapeDtypeStruct((size, size), bf16)
-    return pl.pallas_call(
-        eigen_kernel,
+    vmem = pl.BlockSpec(memory_space=pltpu.VMEM)
+    return pl.pallas_call(
+        end_kernel,
         out_shape=(jax.ShapeDtypeStruct((n, shift_row.shape[1]), f32),) + (table,) * 4,
-        compiler_params=pltpu.CompilerParams(vmem_limit_bytes=32 * 1024 * 1024),
-        cost_estimate=cost(20_000_000_000, 4 * size * size),
-        name="eigen",
-    )(
-        cell[:, None], as_row(cell), face[:, None], as_row(face), as_row(jnp.roll(face, 1)),
-        screening[:, None], as_row(screening), shift_row,
-    )
-
-
-def forward_y_kernel(charge_ref, high_ref, low_ref, out_ref, rows_high, rows_low):
+        in_specs=[vmem] * 5 + [pl.BlockSpec(memory_space=pl.ANY)],
+        out_specs=(vmem,) * 5,
+        compiler_params=pltpu.CompilerParams(vmem_limit_bytes=VMEM),
+        cost_estimate=cost(15_000_000_000, 4 * size * size),
+        name="eigen_end",
+    )(held, as_row(cell), as_row(face), as_row(screening), shift_row, after)
+
+
+def forward_y_kernel(charge_ref, high_ref, low_ref, after_ref, out_ref, rows_high, rows_low):
     @pl.when(pl.program_id(0) == 0)
     def _():
         high, low = split(charge_ref[...].reshape(rows_high.shape))
@@ -214,7 +263,7 @@
     out_ref[...] = result.reshape(out_ref.shape)
 
 
-def forward_y(charge, chunk, high, low, slabs):
+def forward_y(charge, chunk, high, low, slabs, after):
     depth, x_local, width = charge.shape
     rows = x_local // CHUNKS
     part = width // slabs
@@ -226,13 +275,14 @@
             pl.BlockSpec((depth, rows, width), lambda i: (0, chunk, 0)),
             pl.BlockSpec((width, part), lambda i: (0, i)),
             pl.BlockSpec((width, part), lambda i: (0, i)),
+            pl.BlockSpec(memory_space=pl.ANY),
         ],
         out_specs=pl.BlockSpec((1, depth, rows, part), lambda i: (i, 0, 0, 0)),
         scratch_shapes=[pltpu.VMEM((depth * rows, width), bf16)] * 2,
         compiler_params=params(),
         cost_estimate=cost(6 * depth * rows * width * width, 4 * width * width),
         name="forward_y",
-    )(charge, high, low)
+    )(charge, high, low, after)
 
 
 def rise_kernel(first, value_ref, high_ref, low_ref, ratio_ref, *rest):
@@ -288,9 +338,28 @@
     )(value, high, low, ratio, *(() if state is None else state))
 
 
-def link_kernel(x_local, place_ref, ratio_ref, ends_ref, enter_ref, leave_ref):
-    blocks = ends_ref.shape[0]
-    place = place_ref[0]
+def link_kernel(
+    x_local, ratio_ref, ends_ref, enter_ref, leave_ref, held_ref, send_sems, recv_sems
+):
+    blocks = held_ref.shape[0]
+    me = lax.axis_index("gx")
+    barrier = pltpu.get_barrier_semaphore()
+    for step in range(1, blocks):
+        other = lax.rem(me + step, blocks)
+        pl.semaphore_signal(barrier, inc=1, device_id={"gx": other}, device_id_type=MESH)
+    pl.semaphore_wait(barrier, blocks - 1)
+    copies = []
+    for step in range(1, blocks):
+        copy = pltpu.make_async_remote_copy(
+            src_ref=ends_ref,
+            dst_ref=held_ref.at[step],
+            send_sem=send_sems.at[step],
+            recv_sem=recv_sems.at[step],
+            device_id={"gx": lax.rem(me + step, blocks)},
+            device_id_type=MESH,
+        )
+        copy.start()
+        copies.append(copy)
     ratio = ratio_ref[...]
 
     def raised(base, count):
@@ -305,39 +374,46 @@
     across = raised(ratio, x_local)
     around = 1.0 / (1.0 - raised(across, blocks))
     both = ratio * ratio * (1.0 - across * across) / ((1.0 - ratio) * (1.0 + ratio))
-    last = ends_ref[0, 0]
-    for block in range(1, blocks):
-        last = ends_ref[block, 0] + across * last
+    for copy in copies:
+        copy.wait()
+
+    def ends(step, which):
+        return ends_ref[which] if step == 0 else held_ref[step, which]
+
+    last = ends(blocks - 1, 0)
+    for step in reversed(range(blocks - 1)):
+        last = ends(step, 0) + across * last
     last = last * around
     tops = []
-    enter = jnp.zeros_like(last)
-    for block in range(blocks):
-        enter = jnp.where(place == block, last, enter)
-        tops.append(ends_ref[block, 1] + both * last)
-        last = ends_ref[block, 0] + across * last
-    enter_ref[...] = enter
+    for step in reversed(range(blocks)):
+        enter_ref[...] = last
+        tops.append(ends(step, 1) + both * last)
+        last = ends(step, 0) + across * last
     first = tops[-1]
-    for block in reversed(range(blocks - 1)):
-        first = tops[block] + across * first
-    first = first * around
-    leave = jnp.zeros_like(first)
-    for block in reversed(range(blocks)):
-        leave = jnp.where(place == block, first, leave)
-        first = tops[block] + across * first
-    leave_ref[...] = leave
-
-
-def link(place, ratio, gathered, x_local):
+    for top in reversed(tops[:-1]):
+        first = top + across * first
+    leave_ref[...] = first * around
+
+
+def link(ratio, own_ends, x_local, blocks):
     plane = jax.ShapeDtypeStruct(ratio.shape, f32)
     vmem = pl.BlockSpec(memory_space=pltpu.VMEM)
     return pl.pallas_call(
         functools.partial(link_kernel, x_local),
         out_shape=(plane, plane),
-        in_specs=[pl.BlockSpec(memory_space=pltpu.SMEM), vmem, vmem],
+        in_specs=[vmem, vmem],
         out_specs=(vmem, vmem),
-        cost_estimate=cost(10 * gathered.size, 4 * gathered.size),
+        scratch_shapes=[
+            pltpu.VMEM((blocks,) + own_ends.shape, f32),
+            pltpu.SemaphoreType.DMA((blocks,)),
+            pltpu.SemaphoreType.DMA((blocks,)),
+        ],
+        compiler_params=pltpu.CompilerParams(
+            collective_id=0, has_side_effects=True, vmem_limit_bytes=VMEM
+        ),
+        cost_estimate=cost(10 * blocks * own_ends.size, 4 * blocks * own_ends.size),
         name="link",
-    )(place, ratio, gathered)
+    )(ratio, own_ends)
 
 
 def fall_kernel(
@@ -459,22 +535,24 @@
     shift_row = lax.dynamic_slice_in_dim(
         jnp.asarray(mode_shift(width)[None]), lax.axis_index("gz") * part, part, 1
     )
-    place = lax.axis_index("gx").astype(jnp.int32).reshape(1)
     exchange = functools.partial(
         lax.all_to_all, axis_name="gz", split_axis=0, concat_axis=0, tiled=True
     )
-    ratio, to_high, to_low, from_high, from_low = eigen(
-        cell_permittivity, face_permittivity, screening, shift_row
+    layer_values = (cell_permittivity, face_permittivity, screening)
+    sent = [forward_y(charge, 0, fore_high, fore_low, slabs, shift_row)]
+    held = eigen_begin(*layer_values, sent[0])
+    for chunk in range(1, CHUNKS):
+        sent.append(forward_y(charge, chunk, fore_high, fore_low, slabs, held))
+    ratio, to_high, to_low, from_high, from_low = eigen_end(
+        held, *layer_values, shift_row, sent[-1]
     )
     state = None
     risen = []
     for chunk in range(CHUNKS):
-        sent = forward_y(charge, chunk, fore_high, fore_low, slabs)
-        got = exchange(sent).reshape(layers, rows, part)
+        got = exchange(sent[chunk]).reshape(layers, rows, part)
         value, *state = rise(got, to_high, to_low, ratio, state)
         risen.append(value)
-    gathered = lax.all_gather(state[0], "gx", axis=0)
-    enter, leave = link(place, ratio, gathered, x_local)
+    enter, leave = link(ratio, state[0], x_local, lax.axis_size("gx"))
     result = None
     for chunk in reversed(range(CHUNKS)):
         sent, leave = fall(

time: 263 us -> 166 us (0.63)
  Pallas kernels: 139 us -> 90.1 us
  blocking collectives: 28.4 us -> 0 us
  local copies, waits for them, and re-layouts: 21.3 us -> 7.79 us
  starting transfers between devices: 24.3 us -> 19.1 us
    pallas_call x1 -> x2, Pallas kernels: 101 us -> 25.7 us  [the longest x1 15.6 us: eigen_end(): pl.pallas_call(end_kernel, out_shape=(jax.ShapeDtypeStruct((n, shift_row....]
    all_gather x1 -> x0, blocking collectives: 28.4 us -> none  [body(): gathered = lax.all_gather(state[0], 'gx', axis=0)]
    unnamed x42 -> x12, local copies, waits for them, and re-layouts: 19.8 us -> 3.99 us
    pallas_call x1, Pallas kernels: 1.8 us -> 15.1 us  [link(): pl.pallas_call(functools.partial(link_kernel, x_local), out_shape=(plane,...]
    all_to_all x2, starting transfers between devices: 14.3 us -> 9.05 us  [body(): got = exchange(sent.reshape(slabs, depth, rows, part))]
    all_to_all x2, waiting for transfers between devices: 12.9 us -> 7.64 us  [body(): got = exchange(sent[chunk]).reshape(layers, rows, part)]
    pallas_call x2, Pallas kernels: 4.53 us -> 9.67 us  [fall(): pl.pallas_call(functools.partial(fall_kernel, chunk * rows), out_shape=(j...]
    pallas_call x2, Pallas kernels: 5.88 us -> 9.36 us  [rise(): pl.pallas_call(functools.partial(rise_kernel, state is None), out_shape=(...]
  transfers between devices with their start and end apart: 4 -> 4, of which waited for: 3 -> 4; matrix products, arithmetic and copies ran while one was open for 1% -> 2% of each run, Pallas kernels for 45% -> 31%
where the time goes in v1:
time: 166 us; the launch traced here: 163 us
  Pallas kernels  90.1 us (54%)
  waiting for transfers between devices  44.8 us (27%)
  starting transfers between devices  19.1 us (12%)
  local copies, waits for them, and re-layouts  7.79 us (5%)
    all_to_all x2, waiting for transfers between devices, body(): got = exchange(sent.reshape(slabs, depth, rows, part))  37.2 us
    pallas_call x1, Pallas kernels, eigen_end(): pl.pallas_call(end_kernel, out_shape=(jax.ShapeDtypeStruct((n, shift_row....  15.6 us
    pallas_call x2, Pallas kernels, back_y(): pl.pallas_call(back_y_kernel, out_shape=jax.ShapeDtypeStruct((depth, x_lo...  15.2 us
    pallas_call x1, Pallas kernels, link(): pl.pallas_call(functools.partial(link_kernel, x_local), out_shape=(plane,...  15.1 us
    pallas_call x2, Pallas kernels, forward_y(): pl.pallas_call(forward_y_kernel, out_shape=jax.ShapeDtypeStruct((slabs, d...  15 us
    pallas_call x1, Pallas kernels, eigen_begin(): pl.pallas_call(functools.partial(begin_kernel, 2), out_shape=jax.ShapeDty...  10.1 us
    all_to_all x2, starting transfers between devices, body(): got = exchange(sent[chunk]).reshape(layers, rows, part)  10 us
    pallas_call x2, Pallas kernels, fall(): pl.pallas_call(functools.partial(fall_kernel, chunk * rows), out_shape=(j...  9.67 us
  transfers between devices with their start and end apart: 4, of which 4 were waited for; matrix products, arithmetic and copies ran while one was open for 2% of the time, Pallas kernels for 31%

profile of v1, /device:TPU:1, one launch (start us, length us, event | category | flops | bytes accessed | tf_op | source)
XLA Modules:
  0.0 163.2 jit_solution(4454258713313839360)
XLA Ops:
  0.0 1.3 constant_dynamic-slice_fusion.after_ref.shift_row
  1.3 7.5 %forward_y.2.after_ref = f32[4,8,64,256]{3,2,1,0:T(8,128)} custom-call(f32[8,128,1024]{2,1,0:T(8,128)} %charge_ref.3, bf16[1024,1024]{1,0:T(8,128)(2,1)} %constant.22.clone.high_ref, bf16[1024,1024]{1,0:T(8,128)(2,1)} %constant.23.clone.low_ref, f32[1,256]{1,0:T(1,128)} %constant_dynamic-slice_fusion.after_ref.shift_row), custom_call_target="tpu_custom_call" | custom-call | flops 3221225472 | bytes 4194304 | tf_op jit(solution)/shard_map/forward_y/pallas_call | solution.py:270
  8.8 4.4 %all-to-all-start = ((f32[4,8,64,256]{3,2,1,0:T(8,128)}), f32[4,8,64,256]{3,2,1,0:T(8,128)S(1)}, u32[]{:S(2)}, u32[]{:S(2)}) async-start(f32[4,8,64,256]{3,2,1,0:T(8,128)} %forward_y.2.after_ref), calls=%async_computation | async-start | bytes 4194304 | tf_op jit(solution)/shard_map/all_to_all | solution.py:552
  15.7 1.3 pad_bitcast_fusion.2
  17.0 10.1 %eigen_begin.1.after_ref.held_ref = f32[32,128]{1,0:T(8,128)} custom-call(f32[32,1]{1,0:T(8,128)} %copy.11.cell_col, f32[1,128]{1,0:T(1,128)} %get-tuple-element.37.cell_row, f32[32,1]{1,0:T(8,128)} %copy.12.face_col, f32[1,128]{1,0:T(1,128)} %get-tuple-element.36.face_row, f32[1,128]{1,0:T(1,128)} %get-tuple-element.38.low_row, ...), custom_call_target="tpu_custom_call" | custom-call | flops 10000000000 | bytes 16384 | tf_op jit(solution)/shard_map/eigen_begin/pallas_call | solution.py:225
  27.1 7.5 %forward_y.3.after_ref = f32[4,8,64,256]{3,2,1,0:T(8,128)} custom-call(f32[8,128,1024]{2,1,0:T(8,128)} %charge_ref.3, bf16[1024,1024]{1,0:T(8,128)(2,1)} %constant.22.clone.high_ref, bf16[1024,1024]{1,0:T(8,128)(2,1)} %constant.23.clone.low_ref, f32[32,128]{1,0:T(8,128)} %eigen_begin.1.after_ref.held_ref), custom_call_target="tpu_custom_call" | custom-call | flops 3221225472 | bytes 4194304 | tf_op jit(solution)/shard_map/forward_y/pallas_call | solution.py:270
  34.6 3.0 %all-to-all-done = f32[4,8,64,256]{3,2,1,0:T(8,128)S(1)} async-done(((f32[4,8,64,256]{3,2,1,0:T(8,128)}), f32[4,8,64,256]{3,2,1,0:T(8,128)S(1)}, u32[]{:S(2)}, u32[]{:S(2)}) %all-to-all-start) | async-done | bytes 2097184 | tf_op jit(solution)/shard_map/all_to_all | solution.py:552
  37.7 1.3 copy-done.1
  39.0 5.6 %all-to-all-start.1 = ((f32[4,8,64,256]{3,2,1,0:T(8,128)}), f32[4,8,64,256]{3,2,1,0:T(8,128)}, u32[]{:S(2)}, u32[]{:S(2)}) async-start(f32[4,8,64,256]{3,2,1,0:T(8,128)} %forward_y.3.after_ref), calls=%async_computation.1 | async-start | bytes 4194304 | tf_op jit(solution)/shard_map/all_to_all | solution.py:552
  44.6 15.6 %eigen_end.1 = (f32[32,256]{1,0:T(8,128)}, bf16[256,256]{1,0:T(8,128)(2,1)}, bf16[256,256]{1,0:T(8,128)(2,1)}, bf16[256,256]{1,0:T(8,128)(2,1)}, bf16[256,256]{1,0:T(8,128)(2,1)}) custom-call(f32[32,128]{1,0:T(8,128)} %eigen_begin.1.after_ref.held_ref, f32[1,128]{1,0:T(1,128)} %get-tuple-element.37.cell_row, f32[1,128]{1,0:T(1,128)} %get-tuple-element.36.face_row, ...), custom_call_target="tpu_custom_call" | custom-call | flops 15000000512 | bytes 262144 | tf_op jit(solution)/shard_map/eigen_end/pallas_call | solution.py:244
  60.2 4.7 %rise.2 = (f32[64,32,256]{2,1,0:T(8,128)}, f32[2,32,256]{2,1,0:T(8,128)}, f32[32,256]{1,0:T(8,128)}) custom-call(f32[32,64,256]{2,1,0:T(8,128)} %bitcast.15, bf16[256,256]{1,0:T(8,128)(2,1)} %get-tuple-element.20.high_ref, bf16[256,256]{1,0:T(8,128)(2,1)} %get-tuple-element.21.low_ref, f32[32,256]{1,0:T(8,128)} %get-tuple-element.22.ratio_ref), custom_call_target="tpu_custom_call" | custom-call | flops 805306368 | bytes 4194304 | tf_op jit(solution)/shard_map/rise/pallas_call | solution.py:324
  64.9 4.6 %all-to-all-done.1 = f32[4,8,64,256]{3,2,1,0:T(8,128)} async-done(((f32[4,8,64,256]{3,2,1,0:T(8,128)}), f32[4,8,64,256]{3,2,1,0:T(8,128)}, u32[]{:S(2)}, u32[]{:S(2)}) %all-to-all-start.1) | async-done | bytes 2097184 | tf_op jit(solution)/shard_map/all_to_all | solution.py:552
  69.5 4.7 %rise.3 = (f32[64,32,256]{2,1,0:T(8,128)}, f32[2,32,256]{2,1,0:T(8,128)}, f32[32,256]{1,0:T(8,128)}) custom-call(f32[32,64,256]{2,1,0:T(8,128)} %bitcast.7.value_ref, bf16[256,256]{1,0:T(8,128)(2,1)} %get-tuple-element.20.high_ref, bf16[256,256]{1,0:T(8,128)(2,1)} %get-tuple-element.21.low_ref, f32[32,256]{1,0:T(8,128)} %get-tuple-element.22.ratio_ref, ...), custom_call_target="tpu_custom_call" | custom-call | flops 805306368 | bytes 4194304 | tf_op jit(solution)/shard_map/rise/pallas_call | solution.py:324
  74.2 15.1 %link.1 = (f32[32,256]{1,0:T(8,128)}, f32[32,256]{1,0:T(8,128)}) custom-call(f32[32,256]{1,0:T(8,128)} %get-tuple-element.22.ratio_ref, f32[2,32,256]{2,1,0:T(8,128)} %get-tuple-element.28.ends_ref), custom_call_target="tpu_custom_call" | custom-call | flops 1310720 | bytes 524288 | tf_op jit(solution)/shard_map/link/pallas_call | solution.py:401
  89.3 4.8 %fall.2 = (f32[32,64,256]{2,1,0:T(8,128)}, f32[32,256]{1,0:T(8,128)}) custom-call(f32[64,32,256]{2,1,0:T(8,128)} %get-tuple-element.30.value_ref, bf16[256,256]{1,0:T(8,128)(2,1)} %get-tuple-element.24.high_ref, bf16[256,256]{1,0:T(8,128)(2,1)} %get-tuple-element.25.low_ref, f32[32,256]{1,0:T(8,128)} %get-tuple-element.22.ratio_ref, ...), custom_call_target="tpu_custom_call" | custom-call | flops 805306368 | bytes 4194304 | tf_op jit(solution)/shard_map/fall/pallas_call | solution.py:456
  94.1 4.6 %all-to-all-start.3 = ((f32[4,8,64,256]{3,2,1,0:T(8,128)}), f32[4,8,64,256]{3,2,1,0:T(8,128)S(1)}, u32[]{:S(2)}, u32[]{:S(2)}) async-start(f32[4,8,64,256]{3,2,1,0:T(8,128)} %bitcast.17), calls=%async_computation.3 | async-start | bytes 4194304 | tf_op jit(solution)/shard_map/all_to_all | solution.py:561
  98.8 4.8 %fall.3 = (f32[32,64,256]{2,1,0:T(8,128)}, f32[32,256]{1,0:T(8,128)}) custom-call(f32[64,32,256]{2,1,0:T(8,128)} %get-tuple-element.23.value_ref, bf16[256,256]{1,0:T(8,128)(2,1)} %get-tuple-element.24.high_ref, bf16[256,256]{1,0:T(8,128)(2,1)} %get-tuple-element.25.low_ref, f32[32,256]{1,0:T(8,128)} %get-tuple-element.22.ratio_ref, ...), custom_call_target="tpu_custom_call" | custom-call | flops 805306368 | bytes 4194304 | tf_op jit(solution)/shard_map/fall/pallas_call | solution.py:456
  103.6 20.0 %all-to-all-done.3.value_ref = f32[4,8,64,256]{3,2,1,0:T(8,128)S(1)} async-done(((f32[4,8,64,256]{3,2,1,0:T(8,128)}), f32[4,8,64,256]{3,2,1,0:T(8,128)S(1)}, u32[]{:S(2)}, u32[]{:S(2)}) %all-to-all-start.3) | async-done | bytes 2097184 | tf_op jit(solution)/shard_map/all_to_all | solution.py:561
  123.6 1.3 copy-done.2
  124.9 4.4 %all-to-all-start.2 = ((f32[4,8,64,256]{3,2,1,0:T(8,128)}), f32[4,8,64,256]{3,2,1,0:T(8,128)S(1)}, u32[]{:S(2)}, u32[]{:S(2)}) async-start(f32[4,8,64,256]{3,2,1,0:T(8,128)} %bitcast.16), calls=%async_computation.2 | async-start | bytes 4194304 | tf_op jit(solution)/shard_map/all_to_all | solution.py:561
  129.4 7.6 %back_y.2.rest_0_ = f32[8,128,1024]{2,1,0:T(8,128)} custom-call(f32[4,8,64,256]{3,2,1,0:T(8,128)} %copy-done.2, bf16[1024,1024]{1,0:T(8,128)(2,1)} %constant.24.clone.high_ref, bf16[1024,1024]{1,0:T(8,128)(2,1)} %constant.25.clone.low_ref), custom_call_target="tpu_custom_call" | custom-call | flops 3221225472 | bytes 4194304 | tf_op jit(solution)/shard_map/back_y/pallas_call | solution.py:512
  137.0 17.2 %all-to-all-done.2.value_ref = f32[4,8,64,256]{3,2,1,0:T(8,128)S(1)} async-done(((f32[4,8,64,256]{3,2,1,0:T(8,128)}), f32[4,8,64,256]{3,2,1,0:T(8,128)S(1)}, u32[]{:S(2)}, u32[]{:S(2)}) %all-to-all-start.2) | async-done | bytes 2097184 | tf_op jit(solution)/shard_map/all_to_all | solution.py:561
  154.2 1.3 copy-done
  155.5 7.6 %back_y.3 = f32[8,128,1024]{2,1,0:T(8,128)} custom-call(f32[4,8,64,256]{3,2,1,0:T(8,128)} %copy-done, bf16[1024,1024]{1,0:T(8,128)(2,1)} %constant.24.clone.high_ref, bf16[1024,1024]{1,0:T(8,128)(2,1)} %constant.25.clone.low_ref, f32[8,128,1024]{2,1,0:T(8,128)} %back_y.2.rest_0_), custom_call_target="tpu_custom_call", output_to_operand_aliasing={{}: (3, {})} | custom-call | flops 3221225472 | bytes 4194304 | tf_op jit(solution)/shard_map/back_y/pallas_call | solution.py:512
  (13 shorter events, 2.6 us)
Async XLA Ops:
  8.8 4.4 %copy-start.3 = (f32[32]{0:T(128)S(1)}, f32[32]{0:T(128)}, u32[]{:S(2)}) copy-start(f32[32]{0:T(128)} %param.11) | copy-start | bytes 388
  8.8 5.7 %copy-start.4 = (f32[32]{0:T(128)S(1)}, f32[32]{0:T(128)}, u32[]{:S(2)}) copy-start(f32[32]{0:T(128)} %param.10) | copy-start | bytes 388
  8.8 6.4 %copy-start.5 = (f32[32]{0:T(128)S(1)}, f32[32]{0:T(128)}, u32[]{:S(2)}) copy-start(f32[32]{0:T(128)} %param.12) | copy-start | bytes 388
  8.8 28.9 %all-to-all-start = ((f32[4,8,64,256]{3,2,1,0:T(8,128)}), f32[4,8,64,256]{3,2,1,0:T(8,128)S(1)}, u32[]{:S(2)}, u32[]{:S(2)}) async-start(f32[4,8,64,256]{3,2,1,0:T(8,128)} %forward_y.2.after_ref), calls=%async_computation | async-start | bytes 4194304 | tf_op jit(solution)/shard_map/all_to_all | solution.py:552
  37.7 1.3 copy-start.1
  39.0 30.6 %all-to-all-start.1 = ((f32[4,8,64,256]{3,2,1,0:T(8,128)}), f32[4,8,64,256]{3,2,1,0:T(8,128)}, u32[]{:S(2)}, u32[]{:S(2)}) async-start(f32[4,8,64,256]{3,2,1,0:T(8,128)} %forward_y.3.after_ref), calls=%async_computation.1 | async-start | bytes 4194304 | tf_op jit(solution)/shard_map/all_to_all | solution.py:552
  94.1 29.4 %all-to-all-start.3 = ((f32[4,8,64,256]{3,2,1,0:T(8,128)}), f32[4,8,64,256]{3,2,1,0:T(8,128)S(1)}, u32[]{:S(2)}, u32[]{:S(2)}) async-start(f32[4,8,64,256]{3,2,1,0:T(8,128)} %bitcast.17), calls=%async_computation.3 | async-start | bytes 4194304 | tf_op jit(solution)/shard_map/all_to_all | solution.py:561
  123.6 1.3 copy-start.2
  124.9 29.3 %all-to-all-start.2 = ((f32[4,8,64,256]{3,2,1,0:T(8,128)}), f32[4,8,64,256]{3,2,1,0:T(8,128)S(1)}, u32[]{:S(2)}, u32[]{:S(2)}) async-start(f32[4,8,64,256]{3,2,1,0:T(8,128)} %bitcast.16), calls=%async_computation.2 | async-start | bytes 4194304 | tf_op jit(solution)/shard_map/all_to_all | solution.py:561
  154.2 1.3 copy-start
